TPU v7x, 32 devices: a whole 2x2x4 slice. The times are simulated.
32 devices in a mesh: dp: 16 (over z, y, x), seq: 2 (over core).
Axes of the slice: x: 2, y: 2, z: 4, core: 2. Of those that a mesh axis runs over, the one named last changes fastest.
Arguments:
- block_input: bfloat16 [16, 2048, 512], P('dp', 'seq'), may hold values from -6 to 6
- mixer_gain: bfloat16 [512], P(('dp', 'seq')), may hold values from 0.099609375 to 1.8984375
- mixer_bias: bfloat16 [512], P(('dp', 'seq')), may hold values from -3 to 3
- in_proj: bfloat16 [512, 512], P(('dp', 'seq')), may hold values from -0.25 to 0.25
- kernel_param: bfloat16 [512, 192], P(('dp', 'seq')), may hold values from -6 to 6
- skip_gain: bfloat16 [512], P(('dp', 'seq')), may hold values from -4 to 4
- out_proj: bfloat16 [512, 512], P(('dp', 'seq')), may hold values from -0.25 to 0.25
- mlp_gain: bfloat16 [512], P(('dp', 'seq')), may hold values from 0.099609375 to 1.8984375
- mlp_bias: bfloat16 [512], P(('dp', 'seq')), may hold values from -3 to 3
- up_proj: bfloat16 [512, 2048], P(('dp', 'seq')), may hold values from -0.25 to 0.25
- down_proj: bfloat16 [512, 2048], P(('dp', 'seq')), may hold values from -0.125 to 0.125
- out_cotangent: bfloat16 [16, 2048, 512], P('dp', 'seq'), may hold values from -6 to 6
Outputs:
- block_output: bfloat16 [16, 2048, 512], P('dp', 'seq')
- input_grad: float32 [16, 2048, 512], P('dp', 'seq')
- mixer_gain_grad: float32 [512], P(('dp', 'seq'))
- mixer_bias_grad: float32 [512], P(('dp', 'seq'))
- in_proj_grad: float32 [512, 512], P(('dp', 'seq'))
- kernel_param_grad: float32 [512, 192], P(('dp', 'seq'))
- skip_gain_grad: float32 [512], P(('dp', 'seq'))
- out_proj_grad: float32 [512, 512], P(('dp', 'seq'))
- mlp_gain_grad: float32 [512], P(('dp', 'seq'))
- mlp_bias_grad: float32 [512], P(('dp', 'seq'))
- up_proj_grad: float32 [512, 2048], P(('dp', 'seq'))
- down_proj_grad: float32 [512, 2048], P(('dp', 'seq'))
All inputs are finite; a program needn't handle non-finite values.
Results may differ from a plain program's by a relative error of at most 0.014.
Values may be sent and summed in bfloat16 or wider, within the bound.
No kernel may reach another device: no remote copies, remote signals or barrier semaphores. Data moves between devices by JAX's collectives and lax.ppermute only.
A program may use at most 128 MiB of HBM per device.

v0:
```python
import jax
import jax.numpy as jnp
from jax import lax
from jax.sharding import PartitionSpec as P

TAPS = 32
SCALES = 6
FINE = 3


def from_behind(block, axis, distance):
    devices = range(lax.axis_size(axis))
    route = [(i - distance, i) for i in devices if i - distance in devices]
    return lax.ppermute(block, axis, route)


def layer_norm(features, norm_gain, norm_bias):
    centre_val = features - jnp.mean(features, axis=-1, keepdims=True)
    variance = jnp.mean(centre_val * centre_val, axis=-1, keepdims=True)
    return centre_val * lax.rsqrt(variance + 1e-05) * norm_gain + norm_bias


def gelu_exact(values):
    return jax.nn.gelu(values, approximate=False)


def build_kernel(param_rows):
    fine_parts = []
    coarse_parts = []
    for scale_at in range(SCALES):
        columns = param_rows[:, scale_at * TAPS : (scale_at + 1) * TAPS].T
        if scale_at < FINE:
            fine_parts.append(jnp.repeat(columns, 2**scale_at, axis=0) * 0.5**scale_at)
        else:
            coarse_parts.append(jnp.repeat(columns, 2 ** (scale_at - FINE), axis=0) * 0.5**scale_at)
    raw_fine = jnp.concatenate(fine_parts, axis=0)
    raw_coarse = jnp.concatenate(coarse_parts, axis=0)
    squares = jnp.sum(raw_fine * raw_fine, axis=0) + jnp.sum(raw_coarse * raw_coarse, axis=0)
    inverse = lax.rsqrt(squares + 1e-05)
    return (raw_fine * inverse, raw_coarse * inverse)


def tap_sum(source, kernel, start_at, length, stride):

    def group_step(group_at, running):
        for within in range(8):
            tap_at = group_at * 8 + within
            window = lax.dynamic_slice_in_dim(source, start_at + stride * tap_at, length, 1)
            weight_row = lax.dynamic_index_in_dim(kernel, tap_at, 0, False).astype(jnp.float32)
            running = running + window.astype(jnp.float32) * weight_row
        return running

    running = jnp.zeros((source.shape[0], length, source.shape[2]), jnp.float32)
    return lax.fori_loop(0, kernel.shape[0] // 8, group_step, running)


def tap_corr(source, grad_rows, start_at, length, stride, taps_total):

    def group_step(group_at, running):
        tap_sums = []
        for within in range(8):
            tap_at = group_at * 8 + within
            window = lax.dynamic_slice_in_dim(source, start_at + stride * tap_at, length, 1)
            tap_sums.append(
                jnp.sum(window.astype(jnp.float32) * grad_rows.astype(jnp.float32), axis=(0, 1))
            )
        return lax.dynamic_update_slice_in_dim(running, jnp.stack(tap_sums), group_at * 8, 0)

    running = jnp.zeros((taps_total, source.shape[2]), jnp.float32)
    return lax.fori_loop(0, taps_total // 8, group_step, running)


def seq_major(term, dp_count, seq_count):
    rest = term.shape[0] // (dp_count * seq_count)
    shaped = term.reshape((dp_count, seq_count, rest) + term.shape[1:])
    return jnp.swapaxes(shaped, 0, 1).reshape(term.shape)


def body(
    block_input,
    mixer_gain,
    mixer_bias,
    in_proj,
    kernel_param,
    skip_gain,
    out_proj,
    mlp_gain,
    mlp_bias,
    up_proj,
    down_proj,
    out_cotangent,
):
    gain_one, bias_one, proj_in, param_all, skip_all, proj_out = (
        lax.all_gather(mixer_gain, ("dp", "seq"), axis=0, tiled=True),
        lax.all_gather(mixer_bias, ("dp", "seq"), axis=0, tiled=True),
        lax.all_gather(in_proj, ("dp", "seq"), axis=0, tiled=True),
        lax.all_gather(kernel_param, ("dp", "seq"), axis=0, tiled=True),
        lax.all_gather(skip_gain, ("dp", "seq"), axis=0, tiled=True),
        lax.all_gather(out_proj, ("dp", "seq"), axis=0, tiled=True),
    )
    gain_two, bias_two, proj_up, proj_down = (
        lax.all_gather(mlp_gain, ("dp", "seq"), axis=0, tiled=True),
        lax.all_gather(mlp_bias, ("dp", "seq"), axis=0, tiled=True),
        lax.all_gather(up_proj, ("dp", "seq"), axis=0, tiled=True),
        lax.all_gather(down_proj, ("dp", "seq"), axis=0, tiled=True),
    )
    seq_count, seq_block, feat_count = block_input.shape
    fine_reach = TAPS * (2**FINE - 1)
    coarse_reach = TAPS * (2 ** (SCALES - FINE) - 1)
    pool_size = 2**FINE
    pool_offset = fine_reach // pool_size
    pooled_block = seq_block // pool_size
    seq_index = lax.axis_index("seq")
    dp_total = lax.axis_size("dp")
    seq_total = lax.axis_size("seq")
    resid_in = block_input.astype(jnp.float32)
    normed_f, norm_back_one = jax.vjp(
        layer_norm, resid_in, gain_one.astype(jnp.float32), bias_one.astype(jnp.float32)
    )
    normed_in = normed_f.astype(jnp.bfloat16)
    mixed = jnp.einsum(
        "std,de->ste", normed_in, proj_in, preferred_element_type=jnp.float32
    ).astype(jnp.bfloat16)
    (fine_f, coarse_f), kernel_back = jax.vjp(build_kernel, param_all.astype(jnp.float32))
    fine_kernel = fine_f.astype(jnp.bfloat16)
    coarse_kernel = coarse_f.astype(jnp.bfloat16)
    prior = from_behind(mixed[:, seq_block - fine_reach :, :], "seq", 1)
    pooled_local = jnp.mean(
        mixed.astype(jnp.float32).reshape(seq_count, pooled_block, pool_size, feat_count), axis=2
    ).astype(jnp.bfloat16)
    pooled_all = lax.all_gather(pooled_local, "seq", axis=1, tiled=True)
    extended = jnp.concatenate([prior, mixed], axis=1)
    fine_part = tap_sum(extended, fine_kernel, fine_reach, seq_block, -1)
    padded_pool = jnp.pad(pooled_all, ((0, 0), (pool_offset + coarse_reach, 0), (0, 0)))
    coarse_base = coarse_reach + seq_index * pooled_block
    coarse_part = tap_sum(padded_pool, coarse_kernel, coarse_base, pooled_block, -1)
    skip_f = skip_all.astype(jnp.float32)
    pre_act = (
        fine_part + jnp.repeat(coarse_part, pool_size, axis=1) + skip_f * mixed.astype(jnp.float32)
    )
    act_f, gelu_back_one = jax.vjp(gelu_exact, pre_act)
    act = act_f.astype(jnp.bfloat16)
    middle = resid_in + jnp.einsum("ste,ed->std", act, proj_out, preferred_element_type=jnp.float32)
    normed_two, norm_back_two = jax.vjp(
        layer_norm, middle, gain_two.astype(jnp.float32), bias_two.astype(jnp.float32)
    )
    normed_mid = normed_two.astype(jnp.bfloat16)
    up_val = jnp.einsum("std,df->stf", normed_mid, proj_up, preferred_element_type=jnp.float32)
    hidden_f, gelu_back_two = jax.vjp(gelu_exact, up_val)
    hidden = hidden_f.astype(jnp.bfloat16)
    block_output = (
        middle + jnp.einsum("stf,df->std", hidden, proj_down, preferred_element_type=jnp.float32)
    ).astype(jnp.bfloat16)
    down_grad = jnp.einsum("std,stf->df", out_cotangent, hidden, preferred_element_type=jnp.float32)
    grad_hidden = jnp.einsum(
        "std,df->stf", out_cotangent, proj_down, preferred_element_type=jnp.float32
    )
    grad_up = gelu_back_two(grad_hidden)[0].astype(jnp.bfloat16)
    up_grad = jnp.einsum("std,stf->df", normed_mid, grad_up, preferred_element_type=jnp.float32)
    grad_nmid = jnp.einsum("stf,df->std", grad_up, proj_up, preferred_element_type=jnp.float32)
    mid_back, gain_two_grad, bias_two_grad = norm_back_two(grad_nmid)
    grad_mid = out_cotangent.astype(jnp.float32) + mid_back
    mlp_terms = (gain_two_grad, bias_two_grad, up_grad, down_grad)
    gain_r, bias_r, up_r, down_r = (seq_major(term, dp_total, seq_total) for term in mlp_terms)
    mlp_half = (
        lax.psum_scatter(
            gain_r.astype(jnp.bfloat16), "seq", scatter_dimension=0, tiled=True
        ).astype(jnp.float32),
        lax.psum_scatter(
            bias_r.astype(jnp.bfloat16), "seq", scatter_dimension=0, tiled=True
        ).astype(jnp.float32),
        lax.psum_scatter(up_r.astype(jnp.bfloat16), "seq", scatter_dimension=0, tiled=True).astype(
            jnp.float32
        ),
        lax.psum_scatter(
            down_r.astype(jnp.bfloat16), "seq", scatter_dimension=0, tiled=True
        ).astype(jnp.float32),
    )
    mlp_sums = (
        lax.psum_scatter(mlp_half[0], "dp", scatter_dimension=0, tiled=True),
        lax.psum_scatter(mlp_half[1], "dp", scatter_dimension=0, tiled=True),
        lax.psum_scatter(mlp_half[2], "dp", scatter_dimension=0, tiled=True),
        lax.psum_scatter(mlp_half[3], "dp", scatter_dimension=0, tiled=True),
    )
    grad_branch = grad_mid.astype(jnp.bfloat16)
    out_grad = jnp.einsum("ste,std->ed", act, grad_branch, preferred_element_type=jnp.float32)
    grad_act = jnp.einsum("std,ed->ste", grad_branch, proj_out, preferred_element_type=jnp.float32)
    grad_pre = gelu_back_one(grad_act)[0].astype(jnp.bfloat16)
    skip_grad = jnp.sum(grad_pre.astype(jnp.float32) * mixed.astype(jnp.float32), axis=(0, 1))
    padded_grad = jnp.pad(grad_pre, ((0, 0), (fine_reach, fine_reach), (0, 0)))
    ext_grad = tap_sum(padded_grad, fine_kernel, 0, fine_reach + seq_block, 1)
    next_grad = from_behind(ext_grad[:, :fine_reach, :].astype(jnp.bfloat16), "seq", -1).astype(
        jnp.float32
    )
    local_grad = ext_grad[:, fine_reach:, :] + jnp.pad(
        next_grad, ((0, 0), (seq_block - fine_reach, 0), (0, 0))
    )
    fine_kgrad = tap_corr(extended, grad_pre, fine_reach, seq_block, -1, fine_reach)
    grad_cpool = jnp.sum(
        grad_pre.astype(jnp.float32).reshape(seq_count, pooled_block, pool_size, feat_count), axis=2
    )
    coarse_kgrad = tap_corr(padded_pool, grad_cpool, coarse_base, pooled_block, -1, coarse_reach)
    pooled_len = pooled_all.shape[1]
    placed = jnp.zeros(
        (seq_count, pooled_len + pool_offset + coarse_reach, feat_count), jnp.float32
    )
    placed = lax.dynamic_update_slice_in_dim(placed, grad_cpool, seq_index * pooled_block, 1)
    pool_terms = tap_sum(placed, coarse_kernel, pool_offset, pooled_len, 1)
    pool_back = lax.psum_scatter(
        pool_terms.astype(jnp.bfloat16), "seq", scatter_dimension=1, tiled=True
    ).astype(jnp.float32)
    total_grad = (
        local_grad
        + jnp.repeat(pool_back / pool_size, pool_size, axis=1)
        + skip_f * grad_pre.astype(jnp.float32)
    )
    grad_mixed = total_grad.astype(jnp.bfloat16)
    in_grad = jnp.einsum("std,ste->de", normed_in, grad_mixed, preferred_element_type=jnp.float32)
    grad_nin = jnp.einsum("ste,de->std", grad_mixed, proj_in, preferred_element_type=jnp.float32)
    in_back, gain_one_grad, bias_one_grad = norm_back_one(grad_nin)
    input_grad = grad_mid + in_back
    param_grad = kernel_back((fine_kgrad, coarse_kgrad))[0]
    mixer_terms = (gain_one_grad, bias_one_grad, in_grad, param_grad, skip_grad, out_grad)
    g_one, b_one, in_r, param_r, skip_r, out_r = (
        seq_major(term, dp_total, seq_total) for term in mixer_terms
    )
    mixer_half = (
        lax.psum_scatter(g_one.astype(jnp.bfloat16), "seq", scatter_dimension=0, tiled=True).astype(
            jnp.float32
        ),
        lax.psum_scatter(b_one.astype(jnp.bfloat16), "seq", scatter_dimension=0, tiled=True).astype(
            jnp.float32
        ),
        lax.psum_scatter(in_r.astype(jnp.bfloat16), "seq", scatter_dimension=0, tiled=True).astype(
            jnp.float32
        ),
        lax.psum_scatter(
            param_r.astype(jnp.bfloat16), "seq", scatter_dimension=0, tiled=True
        ).astype(jnp.float32),
        lax.psum_scatter(
            skip_r.astype(jnp.bfloat16), "seq", scatter_dimension=0, tiled=True
        ).astype(jnp.float32),
        lax.psum_scatter(out_r.astype(jnp.bfloat16), "seq", scatter_dimension=0, tiled=True).astype(
            jnp.float32
        ),
    )
    mixer_sums = (
        lax.psum_scatter(mixer_half[0], "dp", scatter_dimension=0, tiled=True),
        lax.psum_scatter(mixer_half[1], "dp", scatter_dimension=0, tiled=True),
        lax.psum_scatter(mixer_half[2], "dp", scatter_dimension=0, tiled=True),
        lax.psum_scatter(mixer_half[3], "dp", scatter_dimension=0, tiled=True),
        lax.psum_scatter(mixer_half[4], "dp", scatter_dimension=0, tiled=True),
        lax.psum_scatter(mixer_half[5], "dp", scatter_dimension=0, tiled=True),
    )
    return (
        block_output,
        input_grad,
        mixer_sums[0],
        mixer_sums[1],
        mixer_sums[2],
        mixer_sums[3],
        mixer_sums[4],
        mixer_sums[5],
        mlp_sums[0],
        mlp_sums[1],
        mlp_sums[2],
        mlp_sums[3],
    )


def solution(mesh):
    placed = (
        P("dp", "seq", None),
        P(("dp", "seq")),
        P(("dp", "seq")),
        P(("dp", "seq"), None),
        P(("dp", "seq"), None),
        P(("dp", "seq")),
        P(("dp", "seq"), None),
        P(("dp", "seq")),
        P(("dp", "seq")),
        P(("dp", "seq"), None),
        P(("dp", "seq"), None),
        P("dp", "seq", None),
    )
    return jax.shard_map(
        body,
        mesh=mesh,
        in_specs=placed,
        out_specs=(
            P("dp", "seq", None),
            P("dp", "seq", None),
            P(("dp", "seq")),
            P(("dp", "seq")),
            P(("dp", "seq"), None),
            P(("dp", "seq"), None),
            P(("dp", "seq")),
            P(("dp", "seq"), None),
            P(("dp", "seq")),
            P(("dp", "seq")),
            P(("dp", "seq"), None),
            P(("dp", "seq"), None),
        ),
        check_vma=False,
    )
```

profile of v0, /device:TPU:0, one launch (start us, length us, event | category | flops | bytes accessed | tf_op | source)
XLA Modules:
  0.0 1317.2 jit_solution(17261368303675134988)
XLA Ops:
  12.2 42.1 %all-reduce.25 = (bf16[512]{0:T(512)(128)(2,1)S(1)}, bf16[512]{0:T(512)(128)(2,1)S(1)}, bf16[512]{0:T(512)(128)(2,1)S(1)}, bf16[512]{0:T(512)(128)(2,1)S(1)}, bf16[512]{0:T(512)(128)(2,1)S(1)}) all-reduce(bf16[512]{0:T(512)(128)(2,1)S(1)} %dynamic-update-slice.1, ...), channel_id=1, replica_groups=mesh['dp'=16,'seq'=2] {'dp','seq'}, use_global_device_ids=true, to_apply=%add.10 | all-reduce | flops 2560 | bytes 10240
  56.6 41.6 %all_gather.35 = bf16[512,512]{1,0:T(8,128)(2,1)S(1)} all-gather(bf16[16,512]{1,0:T(8,128)(2,1)S(1)} %copy-done.66), channel_id=1, replica_groups=mesh['dp'=16,'seq'=2] {'dp','seq'}, dimensions={0}, use_global_device_ids=true | all-gather | bytes 540672 | tf_op jit(solution)/shard_map/all_gather | solution.py:96
  105.0 37.1 %all_gather.36 = bf16[512,192]{1,0:T(8,128)(2,1)S(1)} all-gather(bf16[16,192]{1,0:T(8,128)(2,1)S(1)} %copy-done.68), channel_id=1, replica_groups=mesh['dp'=16,'seq'=2] {'dp','seq'}, dimensions={0}, use_global_device_ids=true | all-gather | bytes 202752 | tf_op jit(solution)/shard_map/all_gather | solution.py:97
  147.1 15.8 %while.104 = (s32[]{:T(128)}, f32[1,128,512]{2,1,0:T(8,128)S(1)}, s32[]{:T(128)}, bf16[1,508,512]{2,1,0:T(8,128)(2,1)S(1)}, bf16[224,512]{1,0:T(8,128)(2,1)S(1)}...) while((s32[]{:T(128)}, f32[1,128,512]{2,1,0:T(8,128)S(1)}, ...), condition=%wide.region_8.9_spmd.clone, body=%wide.region_7.8_spmd.clone.sunk | while | flops 1642571 | bytes 1614951 | solution.py:54
  165.4 43.0 %all_gather.39 = bf16[512,512]{1,0:T(8,128)(2,1)} all-gather(bf16[16,512]{1,0:T(8,128)(2,1)S(1)} %copy-done.67), channel_id=1, replica_groups=mesh['dp'=16,'seq'=2] {'dp','seq'}, dimensions={0}, use_global_device_ids=true | all-gather | bytes 540672 | tf_op jit(solution)/shard_map/all_gather | solution.py:99
  209.7 185.2 %while.103 = (s32[]{:T(128)}, f32[1,1024,512]{2,1,0:T(8,128)}, bf16[1,1248,512]{2,1,0:T(8,128)(2,1)S(1)}, bf16[224,512]{1,0:T(8,128)(2,1)}, s32[]{:T(128)}, /*in...) while((s32[]{:T(128)}, f32[1,1024,512]{2,1,0:T(8,128)}, ...), condition=%wide.region_5.6_spmd.clone, body=%wide.region_4.0_spmd.clone.sunk | while | flops 13111371 | bytes 12624991 | solution.py:54
  394.9 7.0 multiply_convert_fusion.1
  405.6 23.4 %multiply_convert_fusion = (bf16[1024,2048]{1,0:T(8,128)(2,1)}, f32[1024,2048]{1,0:T(8,128)}, f32[1024,2048]{1,0:T(8,128)}) fusion(bf16[512,2048]{1,0:T(8,128)(2,1)} %all-gather.4.cloned.1.call-done, bf16[1,1024,512]{1,2,0:T(8,128)(2,1)} %add_convert_fusion.1), kind=kOutput, calls=%fused_computation.125 | convolution fusion | flops 2283798528 | bytes 24117248 | tf_op jit(solution)/shard_map/std,df->stf/dot_general | solution.py:148
  429.0 9.1 add_convert_fusion
  456.9 93.2 %while.102 = (s32[]{:T(128)}, f32[224,512]{1,0:T(8,128)}, bf16[1,1248,512]{2,1,0:T(8,128)(2,1)S(1)}, bf16[1,1024,512]{2,1,0:T(8,128)(2,1)S(1)}, s32[]{:T(128)}, ...) while((s32[]{:T(128)}, f32[224,512]{1,0:T(8,128)}, ...), condition=%wide.region_49.50_spmd, body=%wide.region_40.49_spmd.sunk | while | flops 13103157 | bytes 9519891 | solution.py:70
  551.2 55.9 %while.101 = (s32[]{:T(128)}, f32[224,512]{1,0:T(8,128)}, s32[]{:T(128)}, bf16[1,508,512]{2,1,0:T(8,128)(2,1)S(1)}, f32[1,128,512]{2,1,0:T(8,128)}, /*index=5*/s...) while((s32[]{:T(128)}, f32[224,512]{1,0:T(8,128)}, ...), condition=%wide.region_38.39_spmd, body=%wide.region_29.38_spmd.sunk | while | flops 1568821 | bytes 1393435 | solution.py:70
  610.5 50.2 %while.106 = (s32[]{:T(128)}, f32[1,256,512]{2,1,0:T(8,128)S(1)}, f32[1,508,512]{2,1,0:T(8,128)S(1)}, bf16[224,512]{1,0:T(8,128)(2,1)}, s32[]{:T(128)}, /*index=...) while((s32[]{:T(128)}, f32[1,256,512]{2,1,0:T(8,128)S(1)}, ...), condition=%wide.region_17.18_spmd.clone, body=%wide.region_16.17_spmd.clone.sunk | while | flops 2232387 | bytes 5284967 | solution.py:54
  669.4 209.3 %while.105 = (s32[]{:T(128)}, f32[1,1248,512]{2,1,0:T(8,128)}, bf16[1,1472,512]{2,1,0:T(8,128)(2,1)S(1)}, bf16[224,512]{1,0:T(8,128)(2,1)}, s32[]{:T(128)}, /*in...) while((s32[]{:T(128)}, f32[1,1248,512]{2,1,0:T(8,128)}, ...), condition=%wide.region_14.15_spmd.clone, body=%wide.region_13.14_spmd.clone.sunk | while | flops 15978547 | bytes 15377279 | solution.py:54
  676.4 6.5 fusion.182
  683.9 6.5 fusion.182
  691.5 6.5 fusion.182
  706.6 6.5 fusion.182
  721.7 6.5 fusion.182
  909.6 8.7 reduce-scatter.30.cloned.1.call-done
  939.9 42.6 %all-reduce.24 = (f32[256]{0:T(256)S(1)}, f32[256]{0:T(256)S(1)}, f32[256]{0:T(256)S(1)}, f32[256]{0:T(256)S(1)}, f32[256]{0:T(256)S(1)}) all-reduce(f32[256]{0:T(256)S(1)} %dynamic-slice_convert_fusion.4, f32[256]{0:T(256)S(1)} %get-tuple-element.1141, ...), channel_id=5, replica_groups=mesh['dp'=16,'seq'=2] {'dp'}, use_global_device_ids=true, to_apply=%region_23.24.clone | all-reduce | flops 1280 | bytes 10240
  998.5 75.7 %reduce-scatter.24.cloned.1.call-done = f32[16,512]{1,0:T(8,128)} async-done(((f32[256,512]{1,0:T(8,128)}), f32[16,512]{1,0:T(8,128)}) %reduce-scatter.24.cloned.1.call-update) | async-done | bytes 32784 | tf_op jit(solution)/shard_map/reduce_scatter | solution.py:253
  1074.1 75.7 %reduce-scatter.16.cloned.1.call-done = f32[16,512]{1,0:T(8,128)} async-done(((f32[256,512]{1,0:T(8,128)}), f32[16,512]{1,0:T(8,128)}) %reduce-scatter.16.cloned.1.call-update) | async-done | bytes 32784 | tf_op jit(solution)/shard_map/reduce_scatter | solution.py:250
  1149.9 79.8 %reduce-scatter.28.cloned.1.call-done = f32[16,2048]{1,0:T(8,128)} async-done(((f32[256,2048]{1,0:T(8,128)}), f32[16,2048]{1,0:T(8,128)}) %reduce-scatter.28.cloned.1.call-update) | async-done | bytes 131088 | tf_op jit(solution)/shard_map/reduce_scatter | solution.py:182
  1229.6 80.6 %reduce-scatter.32.cloned.1.call-done = f32[16,2048]{1,0:T(8,128)} async-done(((f32[256,2048]{1,0:T(8,128)}), f32[16,2048]{1,0:T(8,128)}) %reduce-scatter.32.cloned.1.call-update) | async-done | bytes 131088 | tf_op jit(solution)/shard_map/reduce_scatter | solution.py:183
  (714 shorter events, 689.7 us)
Async XLA Ops:
  7.2 398.4 %all-gather.4.cloned.1.call-start = ((), (), s32[]{:S(2)}) async-start(), calls=%async_computation.11 | async-start | bytes 2162688 | tf_op jit(solution)/shard_map/all_gather | solution.py:104
  7.9 421.1 %all-gather.6.cloned.1.call-start = ((), (), s32[]{:S(2)}) async-start(), calls=%async_computation.12 | async-start | bytes 2162688 | tf_op jit(solution)/shard_map/all_gather | solution.py:105
  56.0 345.9 %copy-start.1 = (bf16[1,1024,512]{1,2,0:T(8,128)(2,1)}, bf16[1,1024,512]{1,2,0:T(8,128)(2,1)S(1)}, u32[]{:S(2)}) copy-start(bf16[1,1024,512]{1,2,0:T(8,128)(2,1)S(1)} %copy.86) | copy-start | bytes 3145732
  102.0 106.4 %collective-permute-start = (bf16[1,224,512]{2,1,0:T(8,128)(2,1)}, bf16[1,224,512]{2,1,0:T(8,128)(2,1)}, u32[]{:S(2)}, u32[]{:S(2)}) collective-permute-start(bf16[1,224,512]{2,1,0:T(8,128)(2,1)} %slice.37), channel_id=1, source_target_pairs={{0,1},{2,3},{4,5},{6,7},{8,9},{10,11},{12,13},{14,15},{16,17},{18,... | collective-permute-start | bytes 688136 | tf_op jit(solution)/shard_map/ppermute | solution.py:14
  105.0 776.1 %reduce-scatter.12.cloned.1.call-start = ((), (), s32[]{:S(2)}) async-start(), calls=%async_computation.13 | async-start | bytes 393216 | tf_op jit(solution)/shard_map/reduce_scatter | solution.py:209
  162.9 288.1 %copy-start.58 = (f32[512]{0:T(512)}, f32[512]{0:T(512)S(1)}, u32[]{:S(2)}) copy-start(f32[512]{0:T(512)S(1)} %convert_element_type.1274) | copy-start | bytes 6148
  551.0 56.2 %copy-start.28 = (f32[64,512]{1,0:T(8,128)S(1)}, f32[64,512]{1,0:T(8,128)}, u32[]{:S(2)}) copy-start(f32[64,512]{1,0:T(8,128)} %copy-done.27) | copy-start | bytes 393220
  551.0 56.2 %copy-start.37 = (f32[32,512]{1,0:T(8,128)S(1)}, f32[32,512]{1,0:T(8,128)}, u32[]{:S(2)}) copy-start(f32[32,512]{1,0:T(8,128)} %copy-done.36) | copy-start | bytes 196612
  551.0 56.2 %copy-start.39 = (f32[32,512]{1,0:T(8,128)S(1)}, f32[32,512]{1,0:T(8,128)}, u32[]{:S(2)}) copy-start(f32[32,512]{1,0:T(8,128)} %copy-done.38) | copy-start | bytes 196612
  551.0 57.4 %copy-start.61 = (f32[512]{0:T(512)S(1)}, f32[512]{0:T(512)}, u32[]{:S(2)}) copy-start(f32[512]{0:T(512)} %copy-done.60) | copy-start | bytes 6148
  551.0 57.4 %copy-start.63 = (f32[512]{0:T(512)S(1)}, f32[512]{0:T(512)}, u32[]{:S(2)}) copy-start(f32[512]{0:T(512)} %copy-done.62) | copy-start | bytes 6148
  551.0 57.4 %copy-start.65 = (f32[512]{0:T(512)S(1)}, f32[512]{0:T(512)}, u32[]{:S(2)}) copy-start(f32[512]{0:T(512)} %copy-done.64) | copy-start | bytes 6148
  661.4 239.6 %reduce-scatter.18.cloned.1.call-start = ((), (), s32[]{:S(2)}) async-start(), calls=%async_computation.16 | async-start | bytes 393216 | tf_op jit(solution)/shard_map/reduce_scatter | solution.py:237
  664.9 238.0 %reduce-scatter.22.cloned.1.call-start = ((), (), s32[]{:S(2)}) async-start(), calls=%async_computation.18 | async-start | bytes 786432 | tf_op jit(solution)/shard_map/reduce_scatter | solution.py:243
  669.4 235.3 %reduce-scatter.14.cloned.1.call-start = ((), (), s32[]{:S(2)}) async-start(), calls=%async_computation.14 | async-start | bytes 786432 | tf_op jit(solution)/shard_map/reduce_scatter | solution.py:234
  669.4 213.7 %copy-start.59 = (f32[512]{0:T(512)S(1)}, f32[512]{0:T(512)}, u32[]{:S(2)}) copy-start(f32[512]{0:T(512)} %copy-done.58) | copy-start | bytes 6148
  879.8 3.4 collective-permute-start.1
  887.4 19.2 %reduce-scatter.26.cloned.1.call-start = ((), (), s32[]{:S(2)}) async-start(), calls=%async_computation.20 | async-start | bytes 3145728 | tf_op jit(solution)/shard_map/reduce_scatter | solution.py:172
  893.7 24.6 %reduce-scatter.30.cloned.1.call-start = ((), (), s32[]{:S(2)}) async-start(), calls=%async_computation.22 | async-start | bytes 3145728 | tf_op jit(solution)/shard_map/reduce_scatter | solution.py:175
  901.0 97.5 %reduce-scatter.20.cloned.1.call-start = ((), (), s32[]{:S(2)}) async-start(), calls=%async_computation.17 | async-start | bytes 278528 | tf_op jit(solution)/shard_map/reduce_scatter | solution.py:251
  902.7 171.4 %reduce-scatter.24.cloned.1.call-start = ((), (), s32[]{:S(2)}) async-start(), calls=%async_computation.19 | async-start | bytes 557056 | tf_op jit(solution)/shard_map/reduce_scatter | solution.py:253
  904.7 245.2 %reduce-scatter.16.cloned.1.call-start = ((), (), s32[]{:S(2)}) async-start(), calls=%async_computation.15 | async-start | bytes 557056 | tf_op jit(solution)/shard_map/reduce_scatter | solution.py:250
  906.6 323.1 %reduce-scatter.28.cloned.1.call-start = ((), (), s32[]{:S(2)}) async-start(), calls=%async_computation.21 | async-start | bytes 2228224 | tf_op jit(solution)/shard_map/reduce_scatter | solution.py:182
  909.5 400.7 %reduce-scatter.32.cloned.1.call-start = ((), (), s32[]{:S(2)}) async-start(), calls=%async_computation.23 | async-start | bytes 2228224 | tf_op jit(solution)/shard_map/reduce_scatter | solution.py:183
  (66 other events, 691.7 us)
Sparse Core Ops, SparseCore 0:
  10.9 59.4 all-gather.3
  105.1 52.4 all-gather.5
  661.5 3.7 reduce-scatter.11
  667.5 8.8 reduce-scatter.17
  678.4 9.1 reduce-scatter.21
  887.6 3.8 reduce-scatter.13
  894.3 10.7 reduce-scatter.25
  907.4 10.7 reduce-scatter.29
  921.1 77.3 reduce-scatter.19
  1001.2 72.8 reduce-scatter.23
  1077.0 72.8 reduce-scatter.15
  1152.7 76.9 reduce-scatter.27
  1232.6 77.6 reduce-scatter.31
where the time goes:
time: 1330 us; the launch traced here: 1320 us
  other arithmetic  603 us (45%)
  waiting for transfers between devices  329 us (25%)
  blocking collectives  211 us (16%)
  local copies, waits for them, and re-layouts  81.1 us (6%)
  matrix products  60.1 us (5%)
  between operations  16.9 us (1%)
    add x112, other arithmetic, group_step(): running = running + window.astype(jnp.float32) * weight_row  363 us
    reduce_sum x56, other arithmetic, group_step(): jnp.sum(window.astype(jnp.float32) * grad_rows.astype(jnp.float32), axis=...  112 us
    unnamed x3, blocking collectives  87.2 us
    convert_element_type x112, other arithmetic, group_step(): lax.dynamic_index_in_dim(kernel, tap_at, 0, False).astype(jnp.float32)  85.9 us
    reduce_scatter x1, waiting for transfers between devices, body(): lax.psum_scatter(mlp_half[3], 'dp', scatter_dimension=0, tiled=True)  80.6 us
    reduce_scatter x1, waiting for transfers between devices, body(): lax.psum_scatter(mlp_half[2], 'dp', scatter_dimension=0, tiled=True)  79.8 us
    reduce_scatter x1, waiting for transfers between devices, body(): lax.psum_scatter(mixer_half[2], 'dp', scatter_dimension=0, tiled=True)  75.7 us
    reduce_scatter x1, waiting for transfers between devices, body(): lax.psum_scatter(mixer_half[5], 'dp', scatter_dimension=0, tiled=True)  75.7 us
  transfers between devices with their start and end apart: 15, of which 7 were waited for; matrix products, arithmetic and copies ran while one was open for 39% of the time, Pallas kernels for 0%

commit v1 on v0

v1 whole, which is shorter than its diff:
```python
import math

import jax
import jax.numpy as jnp
import numpy as np
from jax import lax
from jax.sharding import PartitionSpec as P

TAPS = 32
SCALES = 6
FINE = 3
FREQ = 256
BLOCK = 256
POOL = 8
OFFSET = 28
F32 = jnp.float32
BF16 = jnp.bfloat16


def odd_basis(positions):
    angle = np.pi * np.outer(np.arange(FREQ) + 0.5, positions) / FREQ
    return np.concatenate([np.cos(angle), -np.sin(angle)], axis=0)


def tap_basis(first_scale, start):
    columns = []
    for scale_at in range(FINE):
        wide = 2**scale_at
        lag = start + TAPS * (wide - 1)
        for tap in range(TAPS):
            columns.append(odd_basis(lag + tap * wide + np.arange(wide)).sum(axis=1))
    return np.stack(columns, axis=1)


def bf16_const(array):
    return jnp.asarray(np.asarray(array, np.float32).astype(jnp.bfloat16))


def dot(a, b, contract=((1,), (0,))):
    return lax.dot_general(a, b, (contract, ((), ())), preferred_element_type=F32)


def normal_parts(values):
    scaled = values * np.float32(math.sqrt(0.5))
    cdf = 0.5 + 0.5 * lax.erf(scaled)
    pdf = jnp.exp(-scaled * scaled) * np.float32(1 / math.sqrt(2 * math.pi))
    return cdf, pdf


def split_dp(count):
    edge = round((count / 2) ** (1 / 3))
    return (2 * edge, edge * edge) if 2 * edge**3 == count else (1, count)


def swap_route(count, mask):
    return [(i, i ^ mask) for i in range(count)]


def gather_rows(shard):
    dp_count = lax.axis_size("dp")
    nz, nxy = split_dp(dp_count)
    pieces = [shard] + [
        lax.ppermute(shard, "dp", swap_route(dp_count, k * nxy)) for k in range(1, nz)
    ]
    held = jnp.stack(pieces)
    pieces = [held] + [lax.ppermute(held, "dp", swap_route(dp_count, k)) for k in range(1, nxy)]
    held = jnp.stack(pieces)
    held = jnp.stack([held, lax.ppermute(held, "seq", [(0, 1), (1, 0)])])
    me, core = lax.axis_index("dp"), lax.axis_index("seq")
    where = jnp.arange(dp_count) ^ me
    flat = held.reshape((2, dp_count) + shard.shape)
    order = (where % nxy) * nz + where // nxy
    flat = jnp.take(jnp.take(flat, order, axis=1), jnp.arange(2) ^ core, axis=0)
    return jnp.swapaxes(flat, 0, 1).reshape((dp_count * 2 * shard.shape[0],) + shard.shape[1:])


def reduce_rows(term):
    dp_count = lax.axis_size("dp")
    core = lax.axis_index("seq")
    rows = term.shape[0] // (2 * dp_count)
    shaped = term.reshape((dp_count, 2, rows) + term.shape[1:])
    other = lax.dynamic_index_in_dim(shaped, 1 - core, 1, False).astype(BF16)
    mine = lax.dynamic_index_in_dim(shaped, core, 1, False)
    half = (mine + lax.ppermute(other, "seq", [(0, 1), (1, 0)]).astype(F32)).astype(BF16)
    spread = lax.all_to_all(half, "dp", split_axis=0, concat_axis=0, tiled=True)
    return jnp.sum(spread.astype(F32), axis=0)


def normalize(features):
    centre = features - jnp.mean(features, axis=-1, keepdims=True)
    inverse = lax.rsqrt(jnp.mean(centre * centre, axis=-1, keepdims=True) + 1e-05)
    return centre * inverse, inverse


def norm_back(xhat, inverse, scaled):
    return inverse * (
        scaled
        - jnp.mean(scaled, axis=-1, keepdims=True)
        - xhat * jnp.mean(scaled * xhat, axis=-1, keepdims=True)
    )


def halves(spectrum):
    return spectrum[:FREQ], spectrum[FREQ:]


def body(
    block_input,
    mixer_gain,
    mixer_bias,
    in_proj,
    kernel_param,
    skip_gain,
    out_proj,
    mlp_gain,
    mlp_bias,
    up_proj,
    down_proj,
    out_cotangent,
):
    core = lax.axis_index("seq")
    _, length, feats = block_input.shape
    hidden_count = up_proj.shape[1]
    blocks = length // BLOCK
    pooled_len = length // POOL
    x_own = block_input[0]
    cot = out_cotangent[0]
    x_prior = lax.ppermute(x_own, "seq", [(0, 1)])

    vectors = jnp.stack([mixer_gain, mixer_bias, skip_gain, mlp_gain, mlp_bias], axis=1)
    packed = gather_rows(jnp.concatenate([in_proj, kernel_param, vectors], axis=1))
    proj_out = gather_rows(out_proj)
    proj_mlp = gather_rows(jnp.concatenate([up_proj, down_proj], axis=1))
    proj_in = packed[:, :feats]
    param = packed[:, feats : feats + TAPS * SCALES].astype(F32)
    vec = packed[:, feats + TAPS * SCALES :].astype(F32).T
    gain_one, bias_one, skip, gain_two, bias_two = (vec[i : i + 1] for i in range(5))
    proj_up, proj_down = proj_mlp[:, :hidden_count], proj_mlp[:, hidden_count:]

    basis = bf16_const(odd_basis(np.arange(BLOCK)))
    basis_pool = bf16_const(odd_basis(np.arange(-pooled_len, pooled_len)))
    fine_basis = bf16_const(tap_basis(0, 0))
    coarse_basis = bf16_const(tap_basis(FINE, OFFSET))
    sign = jnp.asarray(((-1.0) ** np.arange(FREQ)).astype(np.float32))[:, None]
    pool_rows = np.kron(np.eye(BLOCK // POOL), np.ones((1, POOL)))
    back_pool = bf16_const(
        np.repeat(odd_basis(np.arange(pooled_len)).T, POOL, axis=0)
    )

    tap_scale = jnp.asarray(np.repeat(0.5 ** np.arange(SCALES), TAPS).astype(np.float32))[None]
    tap_wide = jnp.asarray(
        np.repeat(2.0 ** (np.arange(SCALES) % FINE), TAPS).astype(np.float32)
    )[None]

    def taps_of(rows):
        raw = rows * tap_scale
        inverse = lax.rsqrt(jnp.sum(raw * raw * tap_wide, axis=1, keepdims=True) + 1e-05)
        return raw * inverse, inverse

    taps = taps_of(param)[0].astype(BF16)
    fine_h = halves(dot(fine_basis, taps[:, : TAPS * FINE], ((1,), (1,))))
    coarse_h = halves(dot(coarse_basis, taps[:, TAPS * FINE :], ((1,), (1,))))

    xhat, inv_one = normalize(x_own.astype(F32))
    xhat_prior, _ = normalize(x_prior.astype(F32))
    mixed = dot((xhat * gain_one + bias_one).astype(BF16), proj_in).astype(BF16)
    mixed_prior = dot((xhat_prior * gain_one + bias_one).astype(BF16), proj_in).astype(BF16)
    mixed_prior = jnp.where(core > 0, mixed_prior, jnp.zeros_like(mixed_prior))
    mixed_all = jnp.concatenate([mixed_prior, mixed], axis=0)
    pooled = (
        jnp.sum(mixed_all.astype(F32).reshape(2 * pooled_len, POOL, feats), axis=1) / POOL
    ).astype(BF16)

    def span(source, at):
        return source[at * BLOCK : (at + 1) * BLOCK]

    z_mixed = [halves(dot(basis, span(mixed_all, blocks - 1 + at))) for at in range(blocks + 1)]
    window = []
    for at in range(blocks):
        (pr, pi), (zr, zi) = z_mixed[at], z_mixed[at + 1]
        window.append((zr - sign * pi, zi + sign * pr))
    pool_win = halves(dot(basis_pool, pooled))

    def product(h, w):
        return jnp.concatenate([h[0] * w[0] - h[1] * w[1], h[0] * w[1] + h[1] * w[0]]).astype(BF16)

    def conj_product(h, w):
        return jnp.concatenate([h[0] * w[0] + h[1] * w[1], h[0] * w[1] - h[1] * w[0]]).astype(BF16)

    inverse_scale = np.float32(1 / FREQ)
    coarse_y = product(coarse_h, pool_win)
    coarse_part = dot(back_pool, coarse_y)
    fine_part = jnp.concatenate(
        [dot(basis, product(fine_h, window[at]), ((0,), (0,))) for at in range(blocks)]
    )
    mixed_f = mixed.astype(F32)
    pre_act = (fine_part + coarse_part) * inverse_scale + skip * mixed_f
    cdf_one, pdf_one = normal_parts(pre_act)
    act = (pre_act * cdf_one).astype(BF16)
    slope_one = cdf_one + pre_act * pdf_one
    middle = x_own.astype(F32) + dot(act, proj_out)

    xhat_two, inv_two = normalize(middle)
    normed_mid = (xhat_two * gain_two + bias_two).astype(BF16)
    up_val = dot(normed_mid, proj_up)
    cdf_two, pdf_two = normal_parts(up_val)
    hidden = (up_val * cdf_two).astype(BF16)
    block_output = (middle + dot(hidden, proj_down, ((1,), (1,)))).astype(BF16)
    down_grad = dot(cot, hidden, ((0,), (0,)))
    grad_up = (dot(cot, proj_down) * (cdf_two + up_val * pdf_two)).astype(BF16)
    up_grad = dot(normed_mid, grad_up, ((0,), (0,)))
    grad_nmid = dot(grad_up, proj_up, ((1,), (1,)))
    gain_two_grad = jnp.sum(grad_nmid * xhat_two, axis=0)
    bias_two_grad = jnp.sum(grad_nmid, axis=0)
    grad_mid = cot.astype(F32) + norm_back(xhat_two, inv_two, grad_nmid * gain_two)
    mlp_sums = reduce_rows(jnp.concatenate([up_grad, down_grad], axis=1))

    grad_branch = grad_mid.astype(BF16)
    out_grad = dot(act, grad_branch, ((0,), (0,)))
    grad_pre = (dot(grad_branch, proj_out, ((1,), (1,))) * slope_one).astype(BF16)
    grad_cpool = jnp.sum(
        grad_pre.astype(F32).reshape(pooled_len, POOL, feats), axis=1
    ).astype(BF16)
    after = lax.ppermute(
        jnp.concatenate([grad_pre[:BLOCK], grad_cpool], axis=0), "seq", [(1, 0)]
    )
    grad_all = jnp.concatenate([grad_pre, after[:BLOCK]], axis=0)
    z_grad = [halves(dot(basis, span(grad_all, at))) for at in range(blocks + 1)]
    z_pool = halves(dot(basis[:, :pooled_len], grad_cpool))
    z_pool_all = halves(
        dot(basis, jnp.concatenate([grad_cpool, after[BLOCK:]], axis=0))
    )

    def corr(g, w):
        return jnp.concatenate([g[0] * w[0] + g[1] * w[1], g[1] * w[0] - g[0] * w[1]])

    fine_s = sum(corr(z_grad[at], window[at]) for at in range(blocks)).astype(BF16)
    coarse_s = corr(z_pool, pool_win).astype(BF16)
    tap_sums = (
        jnp.concatenate(
            [dot(fine_s, fine_basis, ((0,), (0,))), dot(coarse_s, coarse_basis, ((0,), (0,)))],
            axis=1,
        )
        * inverse_scale
    )
    pieces = []
    for at in range(blocks):
        (zr, zi), (nr, ni) = z_grad[at], z_grad[at + 1]
        pieces.append(
            dot(basis, conj_product(fine_h, (zr + sign * ni, zi - sign * nr)), ((0,), (0,)))
        )
    pool_back = dot(back_pool, conj_product(coarse_h, z_pool_all))
    grad_mixed = (
        (jnp.concatenate(pieces) + pool_back * np.float32(1 / POOL)) * inverse_scale
        + skip * grad_pre.astype(F32)
    ).astype(BF16)
    in_back = dot(xhat.astype(BF16), grad_mixed, ((0,), (0,)))
    mixed_sum = jnp.sum(grad_mixed.astype(F32), axis=0, keepdims=True)
    gain_column, bias_column = gain_one.T, bias_one.T
    in_grad = gain_column * in_back + bias_column * mixed_sum
    proj_in_f = proj_in.astype(F32)
    gain_one_grad = jnp.sum(proj_in_f * in_back, axis=1)
    bias_one_grad = jnp.sum(proj_in_f * mixed_sum, axis=1)
    columns = jnp.stack([gain_one_grad, bias_one_grad, gain_two_grad, bias_two_grad], axis=1)
    mixer_sums = reduce_rows(jnp.concatenate([in_grad, out_grad, tap_sums, columns], axis=1))
    grad_nin = dot(grad_mixed, proj_in, ((1,), (1,)))
    input_grad = grad_mid + norm_back(xhat, inv_one, grad_nin * gain_one)

    tap_rows = mixer_sums[:, 2 * feats : 2 * feats + TAPS * SCALES]
    own_taps, own_inverse = taps_of(kernel_param.astype(F32))
    along = jnp.sum(tap_rows * own_taps, axis=1, keepdims=True)
    param_grad = tap_scale * own_inverse * (tap_rows - tap_wide * own_taps * along)
    tail = mixer_sums[:, 2 * feats + TAPS * SCALES :]
    return (
        block_output[None],
        input_grad[None],
        tail[:, 0],
        tail[:, 1],
        mixer_sums[:, :feats],
        param_grad,
        tap_rows[:, 0],
        mixer_sums[:, feats : 2 * feats],
        tail[:, 2],
        tail[:, 3],
        mlp_sums[:, :hidden_count],
        mlp_sums[:, hidden_count:],
    )


def solution(mesh):
    rows = P(("dp", "seq"), None)
    vector = P(("dp", "seq"))
    tokens = P("dp", "seq", None)
    return jax.shard_map(
        body,
        mesh=mesh,
        in_specs=(
            tokens, vector, vector, rows, rows, vector, rows, vector, vector, rows, rows, tokens,
        ),
        out_specs=(
            tokens, tokens, vector, vector, rows, rows, vector, rows, vector, vector, rows, rows,
        ),
        check_vma=False,
    )
```

time: 1330 us -> 284 us (0.21)
  the two profiles are of different devices: /device:TPU:0 before, /device:TPU:12 now
where the time goes in v1:
time: 284 us; the launch traced here: 280 us
  local copies, waits for them, and re-layouts  67.6 us (24%)
  matrix products  64.7 us (23%)
  waiting for transfers between devices  57.8 us (20%)
  other arithmetic  44.3 us (16%)
  starting transfers between devices  42.8 us (15%)
    dot_general x52, matrix products, dot(): lax.dot_general(a, b, (contract, ((), ())), preferred_element_type=F32)  64.7 us
    all_to_all x2, waiting for transfers between devices, reduce_rows(): spread = lax.all_to_all(half, 'dp', split_axis=0, concat_axis=0, tiled=True)  43.7 us
    gather x10, local copies, waits for them, and re-layouts, gather_rows(): flat = jnp.take(jnp.take(flat, order, axis=1), jnp.arange(2) ^ core, axis=0)  23.3 us
    unnamed x217, local copies, waits for them, and re-layouts  18.1 us
    ppermute x9, starting transfers between devices, gather_rows(): lax.ppermute(shard, 'dp', swap_route(dp_count, k * nxy))  12.7 us
    ppermute x9, waiting for transfers between devices, gather_rows(): lax.ppermute(held, 'dp', swap_route(dp_count, k))  12 us
    all_to_all x2, starting transfers between devices, reduce_rows(): spread = lax.all_to_all(half, 'dp', split_axis=0, concat_axis=0, tiled=True)  11.7 us
    ppermute x9, starting transfers between devices, gather_rows(): lax.ppermute(held, 'dp', swap_route(dp_count, k))  11.1 us
  transfers between devices with their start and end apart: 27, of which 6 were waited for; matrix products, arithmetic and copies ran while one was open for 34% of the time, Pallas kernels for 0%

profile of v1, /device:TPU:12, one launch (start us, length us, event | category | flops | bytes accessed | tf_op | source)
XLA Modules:
  0.0 279.6 jit_solution(3777451465023292265)
XLA Ops:
  8.0 2.7 collective-permute-start.10
  53.5 9.0 %collective-permute-done.19 = bf16[4,16,4096]{2,1,0:T(8,128)(2,1)} collective-permute-done((bf16[4,16,4096]{2,1,0:T(8,128)(2,1)}, bf16[4,16,4096]{2,1,0:T(8,128)(2,1)}, u32[]{:S(2)}, u32[]{:S(2)}) %collective-permute-start.19) | collective-permute-done | bytes 524320 | tf_op jit(solution)/shard_map/ppermute | solution.py:66
  80.1 5.1 %gather_fusion.4 = bf16[16,2,16,4096]{3,2,1,0:T(8,128)(2,1)} fusion(bf16[2,16,16,4096]{3,2,1,0:T(8,128)(2,1)} %pad_maximum_fusion.1, s32[1024]{0:T(1024)} %copy-done.89), kind=kCustom, calls=%fused_computation.4 | custom fusion | bytes 8388672 | tf_op jit(solution)/shard_map/jit(_take)/gather | solution.py:73
  85.2 2.7 select_bitcast_fusion
  91.3 3.7 %gather_fusion.6 = bf16[2,16,16,2048]{3,2,1,0:T(8,128)(2,1)} fusion(bf16[2,16,16,2048]{3,2,1,0:T(8,128)(2,1)} %copy.124, s32[1024]{0:T(1024)} %copy-done.83), kind=kCustom, calls=%fused_computation.6 | custom fusion | bytes 4194312 | tf_op jit(solution)/shard_map/jit(_take)/gather | solution.py:73
  95.0 3.2 %copy.123 = bf16[2,16,16,2048]{3,2,1,0:T(8,128)(2,1)} copy(bf16[2,16,16,2048]{3,2,0,1:T(8,128)(2,1)} %get-tuple-element.77) | data formatting | bytes 4194304 | tf_op jit(solution)/shard_map/jit(_take)/gather | solution.py:73
  98.2 3.8 %gather_fusion.5 = bf16[2,16,16,2048]{3,2,1,0:T(8,128)(2,1)} fusion(bf16[2,16,16,2048]{3,2,1,0:T(8,128)(2,1)} %copy.123, s32[1024]{0:T(1024)} %copy-done.83), kind=kCustom, calls=%fused_computation.5 | custom fusion | bytes 4194312 | tf_op jit(solution)/shard_map/jit(_take)/gather | solution.py:73
  102.0 2.7 fusion.6
  105.4 5.5 %multiply_convert_fusion = (bf16[1024,2048]{1,0:T(8,128)(2,1)}, f32[1024,2048]{1,0:T(8,128)S(1)}) fusion(bf16[512,4096]{1,0:T(8,128)(2,1)S(1)} %bitcast.194, f32[1024,512]{0,1:T(8,128)S(1)} %get-tuple-element.115, f32[512]{0:T(512)S(1)} %copy-done.96, f32[512]{0:T(512)S(1)} %copy-done.78, f32[1024]{0:T(1024)S(1)} %add_rsqrt_fusion, ...), kind=kOutput, calls=%fused_computation.15 | convolution fusion | flops 2160590848 | bytes 16789504 | tf_op jit(solution)/shard_map/dot_general | solution.py:40
  111.0 5.0 %fusion.5 = bf16[1024,2048]{1,0:T(8,128)(2,1)S(1)} fusion(f32[1024,2048]{1,0:T(8,128)S(1)} %get-tuple-element.117, bf16[512,4096]{1,0:T(8,128)(2,1)S(1)} %bitcast.195, bf16[1,1024,512]{2,1,0:T(8,128)(2,1)S(1)} %copy-done.34), kind=kOutput, calls=%fused_computation.13 | convolution fusion | flops 2168455168 | bytes 15728640 | tf_op jit(solution)/shard_map/dot_general | solution.py:40
  116.0 4.3 %fusion.192 = (f32[512]{0:T(512)}, f32[1024,512]{1,0:T(8,128)}) fusion(bf16[1024,2048]{1,0:T(8,128)(2,1)S(1)} %fusion.5, bf16[512,4096]{1,0:T(8,128)(2,1)S(1)} %bitcast.196), kind=kOutput, calls=%fused_computation.353 | convolution fusion | flops 2148007424 | bytes 8390656 | tf_op jit(solution)/shard_map/dot_general | solution.py:40
  120.3 3.4 %copy.129 = f32[1024,512]{0,1:T(8,128)} copy(f32[1024,512]{1,0:T(8,128)} %get-tuple-element.124) | data formatting | bytes 4194304 | tf_op jit(solution)/shard_map/dot_general | solution.py:40
  123.7 3.0 %multiply_reduce_fusion = (f32[512]{0:T(512)}, f32[1024]{0:T(1024)S(1)}, f32[1024]{0:T(1024)S(1)}) fusion(f32[1024,512]{0,1:T(8,128)} %copy.129, f32[1024,512]{0,1:T(8,128)S(1)} %get-tuple-element.115, f32[1024]{0:T(1024)S(1)} %add_rsqrt_fusion, f32[1024]{0:T(1024)S(1)} %broadcast_multiply_fusion.4, f32[512]{0:T(512)} %get-tuple-element.67), kind=kLoop, calls=%fused_computation.73 | loop fusion | flops 4191744 | bytes 4214784 | tf_op jit(solution)/shard_map/reduce_sum | solution.py:213
  141.1 4.5 %fusion.187 = f32[512,2048]{1,0:T(8,128)} fusion(bf16[1024,2048]{1,0:T(8,128)(2,1)S(1)} %copy-done.105, f32[1024,512]{0,1:T(8,128)S(1)} %get-tuple-element.115, f32[512]{0:T(512)S(1)} %copy-done.97, f32[512]{0:T(512)S(1)} %copy-done.79, f32[1024]{0:T(1024)S(1)} %add_rsqrt_fusion, f32[1024]{0:T(1024)S(1)} %broadcast_multiply_fusion.4), kind=kOutput, calls=%fused_computation.348 | convolution fusion | flops 2150105088 | bytes 10498048 | tf_op jit(solution)/shard_map/dot_general | solution.py:40
  156.6 6.9 %convolution_bitcast_fusion = f32[512,2048]{1,0:T(8,128)} fusion(bf16[1024,2048]{1,0:T(8,128)(2,1)} %get-tuple-element.116, bf16[1,1024,512]{2,1,0:T(8,128)(2,1)} %param.31), kind=kOutput, calls=%fused_computation.26 | convolution fusion | flops 2147483648 | bytes 9437184 | tf_op jit(solution)/shard_map/dot_general | solution.py:40
  163.5 4.0 %pad_maximum_fusion = f32[512,4096]{1,0:T(8,128)S(1)} fusion(f32[512,2048]{1,0:T(8,128)} %convolution_bitcast_fusion, f32[512,2048]{1,0:T(8,128)} %fusion.187), kind=kLoop, calls=%fused_computation.14 | loop fusion | flops 2097152 | bytes 16777216 | tf_op jit(solution)/shard_map/concatenate | solution.py:216
  187.4 4.2 %concatenate.138 = f32[16,2,16,1220]{3,2,1,0:T(8,128)} concatenate(f32[16,2,16,512]{3,2,1,0:T(8,128)} %bitcast.212, f32[16,2,16,512]{3,2,1,0:T(8,128)} %bitcast.198, f32[16,2,16,192]{3,2,1,0:T(8,128)} %maximum_multiply_fusion, f32[16,2,16,1]{3,2,1,0:T(8,128)} %concatenate.140, f32[16,2,16,1]{3,2,1,0:T(8,128)} %concatenate.141, f32[16,2,16,1]{3,2,1,0:T(8,128)S(1)} %copy-done.60, ...), dimensions={3} | concatenate | bytes 4997120 | tf_op jit(solution)/shard_map/concatenate | solution.py:265
  197.8 2.5 fusion.55
  200.3 6.2 %all-to-all-start = ((bf16[16,16,1220]{2,1,0:T(8,128)(2,1)}), bf16[16,16,1220]{2,1,0:T(8,128)(2,1)}, u32[]{:S(2)}, u32[]{:S(2)}) async-start(bf16[16,16,1220]{2,1,0:T(8,128)(2,1)} %fusion.55), calls=%async_computation | async-start | bytes 1310720 | tf_op jit(solution)/shard_map/all_to_all | solution.py:85
  206.5 4.8 %fusion.7 = bf16[16,16,4096]{2,1,0:T(8,128)(2,1)} fusion(bf16[16,16,4096]{2,1,0:T(8,128)(2,1)} %collective-permute-done.24, f32[16,2,16,4096]{3,2,1,0:T(8,128)} %bitcast.192, s32[]{:T(128)S(6)} %select_n.152), kind=kLoop, calls=%fused_computation.22 | loop fusion | flops 3145728 | bytes 8388612 | tf_op jit(solution)/shard_map/convert_element_type | solution.py:84
  211.3 12.6 %all-to-all-done = bf16[16,16,1220]{2,1,0:T(8,128)(2,1)} async-done(((bf16[16,16,1220]{2,1,0:T(8,128)(2,1)}), bf16[16,16,1220]{2,1,0:T(8,128)(2,1)}, u32[]{:S(2)}, u32[]{:S(2)}) %all-to-all-start) | async-done | bytes 624672 | tf_op jit(solution)/shard_map/all_to_all | solution.py:85
  223.9 5.5 %all-to-all-start.1 = ((bf16[16,16,4096]{2,1,0:T(8,128)(2,1)}), bf16[16,16,4096]{2,1,0:T(8,128)(2,1)}, u32[]{:S(2)}, u32[]{:S(2)}) async-start(bf16[16,16,4096]{2,1,0:T(8,128)(2,1)} %fusion.7), calls=%async_computation.1 | async-start | bytes 4194304 | tf_op jit(solution)/shard_map/all_to_all | solution.py:85
  229.5 6.2 %fusion.51 = bf16[1,1024,512]{1,2,0:T(8,128)(2,1)} fusion(f32[1024,512]{0,1:T(8,128)S(1)} %get-tuple-element.115, bf16[1024,2048]{1,0:T(8,128)(2,1)} %get-tuple-element.116, bf16[512,4096]{1,0:T(8,128)(2,1)} %bitcast.197), kind=kOutput, calls=%fused_computation.95 | convolution fusion | flops 2148532224 | bytes 9437184 | tf_op jit(solution)/shard_map/dot_general | solution.py:40
  245.7 31.1 %all-to-all-done.1 = bf16[16,16,4096]{2,1,0:T(8,128)(2,1)} async-done(((bf16[16,16,4096]{2,1,0:T(8,128)(2,1)}), bf16[16,16,4096]{2,1,0:T(8,128)(2,1)}, u32[]{:S(2)}, u32[]{:S(2)}) %all-to-all-start.1) | async-done | bytes 2097184 | tf_op jit(solution)/shard_map/all_to_all | solution.py:85
  (392 shorter events, 134.7 us)
Async XLA Ops:
  5.2 14.7 %collective-permute-start.2 = (bf16[16,709]{1,0:T(8,128)(2,1)S(1)}, bf16[16,709]{1,0:T(8,128)(2,1)S(1)}, u32[]{:S(2)}, u32[]{:S(2)}) collective-permute-start(bf16[16,709]{1,0:T(8,128)(2,1)S(1)} %concatenate.107), channel_id=1, source_target_pairs={{0,24},{2,26},{4,28},{6,30},{8,16},{10,18},{12,20},{14,22},{16,8},... | collective-permute-start | bytes 68072 | tf_op jit(solution)/shard_map/ppermute | solution.py:63
  6.8 14.6 %collective-permute-start.1 = (bf16[16,709]{1,0:T(8,128)(2,1)S(1)}, bf16[16,709]{1,0:T(8,128)(2,1)S(1)}, u32[]{:S(2)}, u32[]{:S(2)}) collective-permute-start(bf16[16,709]{1,0:T(8,128)(2,1)S(1)} %concatenate.107), channel_id=1, source_target_pairs={{0,16},{2,18},{4,20},{6,22},{8,24},{10,26},{12,28},{14,30},{16,0},... | collective-permute-start | bytes 68072 | tf_op jit(solution)/shard_map/ppermute | solution.py:63
  8.0 7.9 %collective-permute-start.10 = (bf16[16,512]{1,0:T(8,128)(2,1)}, bf16[16,512]{1,0:T(8,128)(2,1)S(1)}, u32[]{:S(2)}, u32[]{:S(2)}) collective-permute-start(bf16[16,512]{1,0:T(8,128)(2,1)} %param.26), channel_id=1, source_target_pairs={{0,24},{2,26},{4,28},{6,30},{8,16},{10,18},{12,20},{14,22},{16,8},... | collective-permute-start | bytes 49160 | tf_op jit(solution)/shard_map/ppermute | solution.py:63
  10.7 6.6 %collective-permute-start.9 = (bf16[16,512]{1,0:T(8,128)(2,1)}, bf16[16,512]{1,0:T(8,128)(2,1)S(1)}, u32[]{:S(2)}, u32[]{:S(2)}) collective-permute-start(bf16[16,512]{1,0:T(8,128)(2,1)} %param.26), channel_id=1, source_target_pairs={{0,16},{2,18},{4,20},{6,22},{8,24},{10,26},{12,28},{14,30},{16,0},... | collective-permute-start | bytes 49160 | tf_op jit(solution)/shard_map/ppermute | solution.py:63
  11.6 6.7 %collective-permute-start.8 = (bf16[16,512]{1,0:T(8,128)(2,1)}, bf16[16,512]{1,0:T(8,128)(2,1)S(1)}, u32[]{:S(2)}, u32[]{:S(2)}) collective-permute-start(bf16[16,512]{1,0:T(8,128)(2,1)} %param.26), channel_id=1, source_target_pairs={{0,8},{2,10},{4,12},{6,14},{8,0},{10,2},{12,4},{14,6},{16,24},{18,... | collective-permute-start | bytes 49160 | tf_op jit(solution)/shard_map/ppermute | solution.py:63
  15.8 6.1 %collective-permute-start = (bf16[16,709]{1,0:T(8,128)(2,1)S(1)}, bf16[16,709]{1,0:T(8,128)(2,1)S(1)}, u32[]{:S(2)}, u32[]{:S(2)}) collective-permute-start(bf16[16,709]{1,0:T(8,128)(2,1)S(1)} %concatenate.107), channel_id=1, source_target_pairs={{0,8},{2,10},{4,12},{6,14},{8,0},{10,2},{12,4},{14,6},{16,24},{18,... | collective-permute-start | bytes 68072 | tf_op jit(solution)/shard_map/ppermute | solution.py:63
  17.3 17.4 %collective-permute-start.17 = (bf16[16,4096]{1,0:T(8,128)(2,1)S(1)}, bf16[16,4096]{1,0:T(8,128)(2,1)S(1)}, u32[]{:S(2)}, u32[]{:S(2)}) collective-permute-start(bf16[16,4096]{1,0:T(8,128)(2,1)S(1)} %constant_dynamic-update-slice_fusion), channel_id=1, source_target_pairs={{0,24},{2,26},{4,28},{6,30},{8,16},{10,18},{12,20},{14,22},{16,8},... | collective-permute-start | bytes 393224 | tf_op jit(solution)/shard_map/ppermute | solution.py:63
  18.4 6.0 %collective-permute-start.13 = (bf16[4,16,512]{2,1,0:T(8,128)(2,1)S(1)}, bf16[4,16,512]{2,1,0:T(8,128)(2,1)S(1)}, u32[]{:S(2)}, u32[]{:S(2)}) collective-permute-start(bf16[4,16,512]{2,1,0:T(8,128)(2,1)S(1)} %get-tuple-element.111), channel_id=1, source_target_pairs={{0,6},{2,4},{4,2},{6,0},{8,14},{10,12},{12,10},{14,8},{16,22},{18,... | collective-permute-start | bytes 196616 | tf_op jit(solution)/shard_map/ppermute | solution.py:66
  19.9 6.4 %collective-permute-start.12 = (bf16[4,16,512]{2,1,0:T(8,128)(2,1)S(1)}, bf16[4,16,512]{2,1,0:T(8,128)(2,1)S(1)}, u32[]{:S(2)}, u32[]{:S(2)}) collective-permute-start(bf16[4,16,512]{2,1,0:T(8,128)(2,1)S(1)} %get-tuple-element.111), channel_id=1, source_target_pairs={{0,4},{2,6},{4,0},{6,2},{8,12},{10,14},{12,8},{14,10},{16,20},{18,... | collective-permute-start | bytes 196616 | tf_op jit(solution)/shard_map/ppermute | solution.py:66
  21.4 6.2 %collective-permute-start.11 = (bf16[4,16,512]{2,1,0:T(8,128)(2,1)S(1)}, bf16[4,16,512]{2,1,0:T(8,128)(2,1)S(1)}, u32[]{:S(2)}, u32[]{:S(2)}) collective-permute-start(bf16[4,16,512]{2,1,0:T(8,128)(2,1)S(1)} %get-tuple-element.111), channel_id=1, source_target_pairs={{0,2},{2,0},{4,6},{6,4},{8,10},{10,8},{12,14},{14,12},{16,18},{18,... | collective-permute-start | bytes 196616 | tf_op jit(solution)/shard_map/ppermute | solution.py:66
  21.9 6.8 %collective-permute-start.5 = (bf16[4,16,709]{2,1,0:T(8,128)(2,1)S(1)}, bf16[4,16,709]{2,1,0:T(8,128)(2,1)S(1)}, u32[]{:S(2)}, u32[]{:S(2)}) collective-permute-start(bf16[4,16,709]{2,1,0:T(8,128)(2,1)S(1)} %get-tuple-element.107), channel_id=1, source_target_pairs={{0,6},{2,4},{4,2},{6,0},{8,14},{10,12},{12,10},{14,8},{16,22},{18,... | collective-permute-start | bytes 272264 | tf_op jit(solution)/shard_map/ppermute | solution.py:66
  24.4 10.8 %collective-permute-start.16 = (bf16[16,4096]{1,0:T(8,128)(2,1)S(1)}, bf16[16,4096]{1,0:T(8,128)(2,1)S(1)}, u32[]{:S(2)}, u32[]{:S(2)}) collective-permute-start(bf16[16,4096]{1,0:T(8,128)(2,1)S(1)} %constant_dynamic-update-slice_fusion), channel_id=1, source_target_pairs={{0,16},{2,18},{4,20},{6,22},{8,24},{10,26},{12,28},{14,30},{16,0},... | collective-permute-start | bytes 393224 | tf_op jit(solution)/shard_map/ppermute | solution.py:63
  26.3 8.9 %collective-permute-start.15 = (bf16[16,4096]{1,0:T(8,128)(2,1)S(1)}, bf16[16,4096]{1,0:T(8,128)(2,1)S(1)}, u32[]{:S(2)}, u32[]{:S(2)}) collective-permute-start(bf16[16,4096]{1,0:T(8,128)(2,1)S(1)} %constant_dynamic-update-slice_fusion), channel_id=1, source_target_pairs={{0,8},{2,10},{4,12},{6,14},{8,0},{10,2},{12,4},{14,6},{16,24},{18,... | collective-permute-start | bytes 393224 | tf_op jit(solution)/shard_map/ppermute | solution.py:63
  32.2 32.0 %collective-permute-start.7 = (bf16[1024,512]{0,1:T(8,128)(2,1)S(1)}, bf16[1024,512]{0,1:T(8,128)(2,1)S(1)}, u32[]{:S(2)}, u32[]{:S(2)}) collective-permute-start(bf16[1024,512]{0,1:T(8,128)(2,1)S(1)} %bitcast.190), channel_id=1, source_target_pairs={{0,1},{2,3},{4,5},{6,7},{8,9},{10,11},{12,13},{14,15},{16,17},{18,... | collective-permute-start | bytes 3145736 | tf_op jit(solution)/shard_map/ppermute | solution.py:128
  33.8 5.7 %collective-permute-start.14 = (bf16[4,4,16,512]{3,2,1,0:T(8,128)(2,1)S(1)}, bf16[4,4,16,512]{3,2,1,0:T(8,128)(2,1)S(1)}, u32[]{:S(2)}, u32[]{:S(2)}) collective-permute-start(bf16[4,4,16,512]{3,2,1,0:T(8,128)(2,1)S(1)} %pad_maximum_fusion.8), channel_id=1, source_target_pairs={{0,1},{1,0},{2,3},{3,2},{4,5},{5,4},{6,7},{7,6},{8,9},{9,8},{10,11... | collective-permute-start | bytes 786440 | tf_op jit(solution)/shard_map/ppermute | solution.py:68
  34.7 7.4 %collective-permute-start.6 = (bf16[4,4,16,709]{3,2,1,0:T(8,128)(2,1)}, bf16[4,4,16,709]{3,2,1,0:T(8,128)(2,1)}, u32[]{:S(2)}, u32[]{:S(2)}) collective-permute-start(bf16[4,4,16,709]{3,2,1,0:T(8,128)(2,1)} %pad_maximum_fusion.6), channel_id=1, source_target_pairs={{0,1},{1,0},{2,3},{3,2},{4,5},{5,4},{6,7},{7,6},{8,9},{9,8},{10,11... | collective-permute-start | bytes 1089032 | tf_op jit(solution)/shard_map/ppermute | solution.py:68
  36.2 17.3 %collective-permute-start.20 = (bf16[4,16,4096]{2,1,0:T(8,128)(2,1)}, bf16[4,16,4096]{2,1,0:T(8,128)(2,1)}, u32[]{:S(2)}, u32[]{:S(2)}) collective-permute-start(bf16[4,16,4096]{2,1,0:T(8,128)(2,1)} %get-tuple-element.103), channel_id=1, source_target_pairs={{0,6},{2,4},{4,2},{6,0},{8,14},{10,12},{12,10},{14,8},{16,22},{18,... | collective-permute-start | bytes 1572872 | tf_op jit(solution)/shard_map/ppermute | solution.py:66
  38.2 24.3 %collective-permute-start.19 = (bf16[4,16,4096]{2,1,0:T(8,128)(2,1)}, bf16[4,16,4096]{2,1,0:T(8,128)(2,1)}, u32[]{:S(2)}, u32[]{:S(2)}) collective-permute-start(bf16[4,16,4096]{2,1,0:T(8,128)(2,1)} %get-tuple-element.103), channel_id=1, source_target_pairs={{0,4},{2,6},{4,0},{6,2},{8,12},{10,14},{12,8},{14,10},{16,20},{18,... | collective-permute-start | bytes 1572872 | tf_op jit(solution)/shard_map/ppermute | solution.py:66
  39.5 23.0 %collective-permute-start.18 = (bf16[4,16,4096]{2,1,0:T(8,128)(2,1)}, bf16[4,16,4096]{2,1,0:T(8,128)(2,1)}, u32[]{:S(2)}, u32[]{:S(2)}) collective-permute-start(bf16[4,16,4096]{2,1,0:T(8,128)(2,1)} %get-tuple-element.103), channel_id=1, source_target_pairs={{0,2},{2,0},{4,6},{6,4},{8,10},{10,8},{12,14},{14,12},{16,18},{18,... | collective-permute-start | bytes 1572872 | tf_op jit(solution)/shard_map/ppermute | solution.py:66
  64.2 13.6 %collective-permute-start.21 = (bf16[4,4,16,4096]{3,2,1,0:T(8,128)(2,1)S(1)}, bf16[4,4,16,4096]{3,2,1,0:T(8,128)(2,1)S(1)}, u32[]{:S(2)}, u32[]{:S(2)}) collective-permute-start(bf16[4,4,16,4096]{3,2,1,0:T(8,128)(2,1)S(1)} %pad_maximum_fusion.2), channel_id=1, source_target_pairs={{0,1},{1,0},{2,3},{3,2},{4,5},{5,4},{6,7},{7,6},{8,9},{9,8},{10,11... | collective-permute-start | bytes 6291464 | tf_op jit(solution)/shard_map/ppermute | solution.py:68
  146.4 30.9 %collective-permute-start.22 = (bf16[384,512]{1,0:T(8,128)(2,1)}, bf16[384,512]{1,0:T(8,128)(2,1)}, u32[]{:S(2)}, u32[]{:S(2)}) collective-permute-start(bf16[384,512]{1,0:T(8,128)(2,1)} %pad_maximum_fusion.7), channel_id=1, source_target_pairs={{1,0},{3,2},{5,4},{7,6},{9,8},{11,10},{13,12},{15,14},{17,16},{19,... | collective-permute-start | bytes 1179656 | tf_op jit(solution)/shard_map/ppermute | solution.py:224
  169.2 37.3 %collective-permute-start.24 = (bf16[16,16,4096]{2,1,0:T(8,128)(2,1)}, bf16[16,16,4096]{2,1,0:T(8,128)(2,1)}, u32[]{:S(2)}, u32[]{:S(2)}) collective-permute-start(bf16[16,16,4096]{2,1,0:T(8,128)(2,1)} %fusion.37), channel_id=1, source_target_pairs={{0,1},{1,0},{2,3},{3,2},{4,5},{5,4},{6,7},{7,6},{8,9},{9,8},{10,11... | collective-permute-start | bytes 6291464 | tf_op jit(solution)/shard_map/ppermute | solution.py:84
  200.3 23.6 %all-to-all-start = ((bf16[16,16,1220]{2,1,0:T(8,128)(2,1)}), bf16[16,16,1220]{2,1,0:T(8,128)(2,1)}, u32[]{:S(2)}, u32[]{:S(2)}) async-start(bf16[16,16,1220]{2,1,0:T(8,128)(2,1)} %fusion.55), calls=%async_computation | async-start | bytes 1310720 | tf_op jit(solution)/shard_map/all_to_all | solution.py:85
  223.9 52.9 %all-to-all-start.1 = ((bf16[16,16,4096]{2,1,0:T(8,128)(2,1)}), bf16[16,16,4096]{2,1,0:T(8,128)(2,1)}, u32[]{:S(2)}, u32[]{:S(2)}) async-start(bf16[16,16,4096]{2,1,0:T(8,128)(2,1)} %fusion.7), calls=%async_computation.1 | async-start | bytes 4194304 | tf_op jit(solution)/shard_map/all_to_all | solution.py:85
  (109 other events, 586.4 us)
